TPU v7x, 256 devices: a whole 4x4x8 slice. The times are simulated.
256 devices in a mesh: row: 16 (over y_lo, x, core), col: 16 (over z, y_hi).
Axes of the slice: x: 4, y: 4 (y_hi: 2, y_lo: 2; y = y_hi * 2 + y_lo), z: 8, core: 2. Of those that a mesh axis runs over, the one named last changes fastest.
Arguments:
- tokens: int32 [1024], replicated, may hold values from 0 to 16383
- table: bfloat16 [16384, 12288], P('row', 'col'), may hold values from -6 to 6
- gate_weight: bfloat16 [12288, 14336], P('col', 'row'), may hold values from -0.0546875 to 0.0546875
- up_weight: bfloat16 [12288, 14336], P('col', 'row'), may hold values from -0.0546875 to 0.0546875
- down_weight: bfloat16 [14336, 12288], P('row', 'col'), may hold values from -0.046875 to 0.046875
- gate_left: bfloat16 [12288, 64], P(('col', 'row')), may hold values from -0.0546875 to 0.0546875
- gate_right: bfloat16 [64, 14336], P(None, ('row', 'col')), may hold values from -0.3125 to 0.3125
- up_left: bfloat16 [12288, 64], P(('col', 'row')), may hold values from -0.0546875 to 0.0546875
- up_right: bfloat16 [64, 14336], P(None, ('row', 'col')), may hold values from -0.3125 to 0.3125
- down_left: bfloat16 [14336, 64], P(('row', 'col')), may hold values from -0.046875 to 0.046875
- down_right: bfloat16 [64, 12288], P(None, ('col', 'row')), may hold values from -0.3125 to 0.3125
Outputs:
- canary: float32 [1024, 12288], P('row', 'col')
- merged_gate: bfloat16 [12288, 14336], P('col', 'row')
- merged_up: bfloat16 [12288, 14336], P('col', 'row')
- merged_down: bfloat16 [14336, 12288], P('row', 'col')
All inputs are finite; a program needn't handle non-finite values.
Results may differ from a plain program's by a relative error of at most 0.0065.
Values may be sent and summed in bfloat16 or wider, within the bound.
No kernel may reach another device: no remote copies, remote signals or barrier semaphores. Data moves between devices by JAX's collectives and lax.ppermute only.
A program may use at most 64 MiB of HBM per device.

v0:
```python
import jax
import jax.numpy as jnp
from jax import lax
from jax.sharding import PartitionSpec as P


def merge_tile(weight, left, right):
    delta = jnp.dot(left, right, preferred_element_type=jnp.float32)
    return (weight.astype(jnp.float32) + 2.0 * delta).astype(jnp.bfloat16)


def per_device(
    tokens,
    table,
    gate_weight,
    up_weight,
    down_weight,
    gate_left,
    gate_right,
    up_left,
    up_right,
    down_left,
    down_right,
):
    vocab_rows = table.shape[0]
    offset = lax.axis_index("row") * vocab_rows
    local_ids = tokens - offset
    inside = (local_ids >= 0) & (local_ids < vocab_rows)
    picked = jnp.take(table, jnp.clip(local_ids, 0, vocab_rows - 1), axis=0)
    term = jnp.where(inside[:, None], picked, jnp.zeros((), picked.dtype))
    embedded = lax.psum(term, "row").astype(jnp.float32).astype(jnp.bfloat16)
    gate_l, up_l, down_r = (
        lax.all_gather(gate_left, "row", axis=0, tiled=True),
        lax.all_gather(up_left, "row", axis=0, tiled=True),
        lax.all_gather(down_right, "row", axis=1, tiled=True),
    )
    gate_r, up_r, down_l = (
        lax.all_gather(gate_right, "col", axis=1, tiled=True),
        lax.all_gather(up_right, "col", axis=1, tiled=True),
        lax.all_gather(down_left, "col", axis=0, tiled=True),
    )
    merged_gate = merge_tile(gate_weight, gate_l, gate_r)
    merged_up = merge_tile(up_weight, up_l, up_r)
    merged_down = merge_tile(down_weight, down_l, down_r)
    gate_part = jnp.dot(embedded, merged_gate, preferred_element_type=jnp.float32)
    up_part = jnp.dot(embedded, merged_up, preferred_element_type=jnp.float32)
    gate, up = lax.psum((gate_part, up_part), "col")
    hidden = (jax.nn.silu(gate) * up).astype(jnp.bfloat16)
    result = lax.psum_scatter(
        jnp.dot(hidden, merged_down, preferred_element_type=jnp.float32),
        "row",
        scatter_dimension=0,
        tiled=True,
    )
    return (result, merged_gate, merged_up, merged_down)


def solution(mesh):
    in_specs = (
        P(),
        P("row", "col"),
        P("col", "row"),
        P("col", "row"),
        P("row", "col"),
        P(("col", "row"), None),
        P(None, ("row", "col")),
        P(("col", "row"), None),
        P(None, ("row", "col")),
        P(("row", "col"), None),
        P(None, ("col", "row")),
    )
    out_specs = (P("row", "col"), P("col", "row"), P("col", "row"), P("row", "col"))
    return jax.shard_map(
        per_device, mesh=mesh, in_specs=in_specs, out_specs=out_specs, check_vma=False
    )
```

profile of v0, /device:TPU:32, one launch (start us, length us, event | category | flops | bytes accessed | tf_op | source)
XLA Modules:
  0.0 571.8 jit_solution(10741777568530431228)
XLA Ops:
  7.2 0.0 all-reduce.4.cloned.1.call-start
  7.2 0.8 compare_and_fusion.1
  8.0 0.7 fusion.1
  8.7 4.0 gather_fusion
  12.8 1.7 select_select_fusion
  14.5 0.0 all-reduce.6.cloned.1.call-start
  14.5 0.6 copy-done.9
  15.1 20.2 %all_gather.18 = bf16[768,64]{1,0:T(8,128)(2,1)S(1)} all-gather(bf16[48,64]{1,0:T(8,128)(2,1)S(1)} %copy-done.9), channel_id=1, replica_groups=mesh['row'=16,'col'=16] {'row'}, dimensions={0}, use_global_device_ids=true | all-gather | bytes 104448 | tf_op jit(solution)/shard_map/all_gather | solution.py:33
  35.4 16.8 %all_gather.20 = bf16[768,64]{1,0:T(8,128)(2,1)S(1)} all-gather(bf16[48,64]{1,0:T(8,128)(2,1)S(1)} %copy-done.10), channel_id=1, replica_groups=mesh['row'=16,'col'=16] {'row'}, dimensions={0}, use_global_device_ids=true | all-gather | bytes 104448 | tf_op jit(solution)/shard_map/all_gather | solution.py:34
  52.1 42.6 %all_gather.19 = bf16[64,896]{0,1:T(8,128)(2,1)S(1)} all-gather(bf16[64,56]{0,1:T(8,128)(2,1)S(1)} %copy-done.6), channel_id=1, replica_groups=mesh['row'=16,'col'=16] {'col'}, dimensions={1}, use_global_device_ids=true | all-gather | bytes 121856 | tf_op jit(solution)/shard_map/all_gather | solution.py:38
  94.7 37.0 %all_gather.21 = bf16[64,896]{0,1:T(8,128)(2,1)S(1)} all-gather(bf16[64,56]{0,1:T(8,128)(2,1)S(1)} %copy-done.7), channel_id=1, replica_groups=mesh['row'=16,'col'=16] {'col'}, dimensions={1}, use_global_device_ids=true | all-gather | bytes 121856 | tf_op jit(solution)/shard_map/all_gather | solution.py:39
  131.8 1.6 add_convert_fusion.2
  133.4 1.6 add_convert_fusion.1
  135.0 9.0 %all-reduce.4.cloned.1.call-done = bf16[1024,768]{1,0:T(8,128)(2,1)} async-done(((bf16[1024,768]{1,0:T(8,128)(2,1)}), bf16[1024,768]{1,0:T(8,128)(2,1)}) %all-reduce.4.cloned.1.call-update) | async-done | bytes 1572880 | tf_op jit(solution)/shard_map/psum | solution.py:31
  144.0 5.2 fusion.3
  149.2 3.7 fusion.4
  152.9 0.0 reduce-scatter.2.cloned.1.call-start
  153.0 0.6 copy-done.11
  153.6 16.8 %all_gather.23 = bf16[64,768]{0,1:T(8,128)(2,1)S(1)} all-gather(bf16[64,48]{0,1:T(8,128)(2,1)S(1)} %copy-done.11), channel_id=1, replica_groups=mesh['row'=16,'col'=16] {'row'}, dimensions={1}, use_global_device_ids=true | all-gather | bytes 104448 | tf_op jit(solution)/shard_map/all_gather | solution.py:35
  170.4 47.1 %all_gather.22 = bf16[896,64]{1,0:T(8,128)(2,1)S(1)} all-gather(bf16[56,64]{1,0:T(8,128)(2,1)S(1)} %copy-done.8), channel_id=1, replica_groups=mesh['row'=16,'col'=16] {'col'}, dimensions={0}, use_global_device_ids=true | all-gather | bytes 121856 | tf_op jit(solution)/shard_map/all_gather | solution.py:40
  217.5 1.6 add_convert_fusion
  219.1 269.6 %all-reduce.6.cloned.1.call-done = (f32[1024,896]{1,0:T(8,128)}, f32[1024,896]{1,0:T(8,128)}) async-done(((f32[1024,896]{1,0:T(8,128)}, f32[1024,896]{1,0:T(8,128)}), (f32[1024,896]{1,0:T(8,128)}, f32[1024,896]{1,0:T(8,128)})) %all-reduce.6.cloned.1.call-update) | async-done | bytes 7340048 | tf_op jit(solution)/shard_map/psum | solution.py:47
  488.8 7.4 %fusion = f32[1024,768]{1,0:T(8,128)} fusion(bf16[896,768]{1,0:T(8,128)(2,1)} %add_convert_fusion, f32[1024,896]{1,0:T(8,128)} %get-tuple-element.4, f32[1024,896]{1,0:T(8,128)} %get-tuple-element.5), kind=kOutput, calls=%fused_computation.5 | convolution fusion | flops 1414791168 | bytes 11862016 | tf_op jit(solution)/shard_map/dot_general | solution.py:50
  496.2 69.1 %reduce-scatter.2.cloned.1.call-done = f32[64,768]{1,0:T(8,128)} async-done(((f32[1024,768]{1,0:T(8,128)}), f32[64,768]{1,0:T(8,128)}) %reduce-scatter.2.cloned.1.call-update) | async-done | bytes 196624 | tf_op jit(solution)/shard_map/reduce_scatter | solution.py:49
  (27 shorter events, 0.1 us)
Async XLA Ops:
  7.2 1.6 copy-start
  7.2 136.8 %all-reduce.4.cloned.1.call-start = ((), (), s32[]{:S(2)}) async-start(), calls=%async_computation.1 | async-start | bytes 3145728 | tf_op jit(solution)/shard_map/psum | solution.py:31
  14.4 0.7 copy-start.9
  14.4 20.9 %copy-start.10 = (bf16[48,64]{1,0:T(8,128)(2,1)S(1)}, bf16[48,64]{1,0:T(8,128)(2,1)}, u32[]{:S(2)}) copy-start(bf16[48,64]{1,0:T(8,128)(2,1)} %param.18) | copy-start | bytes 18436
  14.4 37.7 %copy-start.6 = (bf16[64,56]{0,1:T(8,128)(2,1)S(1)}, bf16[64,56]{0,1:T(8,128)(2,1)}, u32[]{:S(2)}) copy-start(bf16[64,56]{0,1:T(8,128)(2,1)} %param.17) | copy-start | bytes 21508
  14.4 80.3 %copy-start.7 = (bf16[64,56]{0,1:T(8,128)(2,1)S(1)}, bf16[64,56]{0,1:T(8,128)(2,1)}, u32[]{:S(2)}) copy-start(bf16[64,56]{0,1:T(8,128)(2,1)} %param.19) | copy-start | bytes 21508
  14.4 117.3 %copy-start.1 = (bf16[768,896]{1,0:T(8,128)(2,1)S(1)}, bf16[768,896]{1,0:T(8,128)(2,1)}, u32[]{:S(2)}) copy-start(bf16[768,896]{1,0:T(8,128)(2,1)} %param.13) | copy-start | bytes 4128772
  14.5 474.3 %all-reduce.6.cloned.1.call-start = ((), (), s32[]{:S(2)}) async-start(), calls=%async_computation.3 | async-start | bytes 14680064 | tf_op jit(solution)/shard_map/psum | solution.py:47
  131.8 1.6 copy-start.2
  133.4 10.6 %copy-start.4 = (bf16[768,896]{1,0:T(8,128)(2,1)S(1)}, bf16[768,896]{1,0:T(8,128)(2,1)}, u32[]{:S(2)}) copy-start(bf16[768,896]{1,0:T(8,128)(2,1)} %add_convert_fusion.2) | copy-start | bytes 4128772
  144.0 5.2 copy-start.5
  144.0 5.2 copy-start.12
  152.9 0.7 copy-start.11
  152.9 17.5 %copy-start.8 = (bf16[56,64]{1,0:T(8,128)(2,1)S(1)}, bf16[56,64]{1,0:T(8,128)(2,1)}, u32[]{:S(2)}) copy-start(bf16[56,64]{1,0:T(8,128)(2,1)} %param.20) | copy-start | bytes 21508
  152.9 64.6 %copy-start.3 = (bf16[896,768]{1,0:T(8,128)(2,1)S(1)}, bf16[896,768]{1,0:T(8,128)(2,1)}, u32[]{:S(2)}) copy-start(bf16[896,768]{1,0:T(8,128)(2,1)} %param.15) | copy-start | bytes 4128772
  152.9 412.3 %reduce-scatter.2.cloned.1.call-start = ((), (), s32[]{:S(2)}) async-start(), calls=%async_computation.2 | async-start | bytes 3342336 | tf_op jit(solution)/shard_map/reduce_scatter | solution.py:49
Sparse Core Ops, SparseCore 0:
  14.6 129.3 all-reduce.3
  153.1 335.6 all-reduce.5
  496.3 68.8 reduce-scatter.1
where the time goes:
time: 572 us
  waiting for transfers between devices  348 us (61%)
  blocking collectives  181 us (32%)
  matrix products  21.1 us (4%)
  between operations  13.8 us (2%)
    psum x1, waiting for transfers between devices, per_device(): gate, up = lax.psum((gate_part, up_part), 'col')  270 us
    reduce_scatter x1, waiting for transfers between devices, per_device(): lax.psum_scatter(jnp.dot(hidden, merged_down, preferred_element_type=jnp....  69.1 us
    all_gather x1, blocking collectives, per_device(): lax.all_gather(down_left, 'col', axis=0, tiled=True)  47.1 us
    all_gather x1, blocking collectives, per_device(): lax.all_gather(gate_right, 'col', axis=1, tiled=True)  42.6 us
    all_gather x1, blocking collectives, per_device(): lax.all_gather(up_right, 'col', axis=1, tiled=True)  37 us
    all_gather x1, blocking collectives, per_device(): lax.all_gather(gate_left, 'row', axis=0, tiled=True)  20.2 us
    all_gather x1, blocking collectives, per_device(): lax.all_gather(down_right, 'row', axis=1, tiled=True)  16.8 us
    all_gather x1, blocking collectives, per_device(): lax.all_gather(up_left, 'row', axis=0, tiled=True)  16.8 us
  transfers between devices with their start and end apart: 3, of which 3 were waited for; matrix products, arithmetic and copies ran while one was open for 1% of the time, Pallas kernels for 0%

commit v1 on v0

v1 whole, which is shorter than its diff:
```python
import jax
import jax.numpy as jnp
from jax import lax
from jax.sharding import PartitionSpec as P

BF16 = jnp.bfloat16
F32 = jnp.float32

NX, NZ, NB = 4, 8, 16
CHUNKS = 1


def row_perm(dy=0, dx=0, dc=0):
    return [
        (
            (y * NX + x) * 2 + c,
            ((y ^ dy) * NX + (x + dx) % NX) * 2 + (c ^ dc),
        )
        for y in range(2)
        for x in range(NX)
        for c in range(2)
    ]


def col_perm(dz=0, dy=0):
    return [
        (z * 2 + y, ((z + dz) % NZ) * 2 + (y ^ dy)) for z in range(NZ) for y in range(2)
    ]


def xor_perm(mask):
    return [(i, i ^ mask) for i in range(NB)]


def send_row(value, **kw):
    return lax.ppermute(value, "row", row_perm(**kw))


def send_col(value, **kw):
    return lax.ppermute(value, "col", col_perm(**kw))


def gather_small(piece, axis):
    index = lax.axis_index(axis)
    held = piece[None]
    for bit in range(4):
        other = lax.ppermute(held, axis, xor_perm(1 << bit))
        low = (index >> bit) & 1 == 0
        held = jnp.concatenate(
            [jnp.where(low, held, other), jnp.where(low, other, held)], axis=0
        )
    return held


def merge_tile(weight, left, right):
    delta = jnp.dot(left, right, preferred_element_type=F32)
    return (weight.astype(F32) + 2.0 * delta).astype(BF16)


def lookup(ids, table):
    vocab = table.shape[0]
    local = ids - lax.axis_index("row") * vocab
    hot = (local[:, None] == lax.broadcasted_iota(jnp.int32, (1, vocab), 1)).astype(BF16)
    return jnp.dot(hot, table, preferred_element_type=F32).astype(BF16)


def embed(ids, table):
    n = ids.shape[0]
    m = n // NB
    term = lookup(ids, table)
    half = term[: n // 2] + send_row(term[n // 2 :], dc=1)
    q = n // 8
    parts = [half[:q]] + [
        send_row(half[d * q : (d + 1) * q], dx=d) for d in range(1, NX)
    ]
    mine = parts[0] + parts[1] + parts[2] + parts[3]
    other = send_row(mine, dy=1)
    mine = mine + jnp.concatenate([other[m:], other[:m]], axis=0)
    half = jnp.concatenate(
        [mine] + [send_row(mine, dx=-d) for d in range(1, NX)], axis=0
    )
    return jnp.concatenate([half, send_row(half, dc=1)], axis=0)


def block(value, index, size):
    return lax.dynamic_slice_in_dim(value, (index % NZ) * size, size, axis=0)


def ring_scatter(part, z, sign):
    b = part.shape[0] // NZ
    far = block(part, z + 4 * sign, b).astype(BF16)
    up = send_col(far, dz=sign)
    down = None
    for d in (3, 2, 1):
        up_next = (block(part, z + d * sign, b) + up).astype(BF16)
        mine = block(part, z - d * sign, b)
        down_next = (mine if down is None else mine + down).astype(BF16)
        up = send_col(up_next, dz=sign)
        down = send_col(down_next, dz=-sign)
    return block(part, z, b) + up + down


def ring_gather(piece, z, sign):
    b = piece.shape[0]
    out = jnp.zeros((NZ * b,) + piece.shape[1:], piece.dtype)

    def put(out, value, index):
        return lax.dynamic_update_slice_in_dim(out, value, (index % NZ) * b, axis=0)

    out = put(out, piece, z)
    up = down = piece
    for d in (1, 2, 3):
        up = send_col(up, dz=sign)
        down = send_col(down, dz=-sign)
        out = put(out, up, z - d * sign)
        out = put(out, down, z + d * sign)
    up = send_col(up, dz=sign)
    return put(out, up, z - 4 * sign)


def activate(total):
    w = total.shape[1] // 2
    gate, up = total[:, :w], total[:, w:]
    return (jax.nn.silu(gate) * up).astype(BF16)


def swiglu_z_first(part, z, y, sign):
    m = part.shape[0] // NB
    both = ring_scatter(part, z, sign)
    theirs = lax.dynamic_slice_in_dim(both, (1 - y) * m, m, axis=0).astype(BF16)
    mine = lax.dynamic_slice_in_dim(both, y * m, m, axis=0)
    hidden = activate(mine + send_col(theirs, dy=1))
    other = send_col(hidden, dy=1)
    low = y == 0
    pair = jnp.concatenate(
        [jnp.where(low, hidden, other), jnp.where(low, other, hidden)], axis=0
    )
    return ring_gather(pair, z, sign)


def swiglu_y_first(part, z, y, sign):
    h = part.shape[0] // 2
    theirs = lax.dynamic_slice_in_dim(part, (1 - y) * h, h, axis=0).astype(BF16)
    mine = lax.dynamic_slice_in_dim(part, y * h, h, axis=0)
    mine = mine + send_col(theirs, dy=1)
    hidden = ring_gather(activate(ring_scatter(mine, z, sign)), z, sign)
    other = send_col(hidden, dy=1)
    low = y == 0
    return jnp.concatenate(
        [jnp.where(low, hidden, other), jnp.where(low, other, hidden)], axis=0
    )


def scatter_rows(part):
    n = part.shape[0]
    m, q = n // NB, n // 8
    half = part[: n // 2] + send_row(part[n // 2 :].astype(BF16), dc=1)
    parts = [half[:q]] + [
        send_row(half[d * q : (d + 1) * q].astype(BF16), dx=d) for d in range(1, NX)
    ]
    mine = parts[0] + parts[1] + parts[2] + parts[3]
    return mine[:m] + send_row(mine[m:].astype(BF16), dy=1)


def relative_tokens(tokens):
    row = lax.axis_index("row")
    core, x, y = row % 2, (row // 2) % NX, row // (2 * NX)
    m = tokens.shape[0] // (NB * CHUNKS)
    ids = tokens.reshape(2, NX, 2, CHUNKS, m)
    order = (jnp.arange(2) + y) % 2
    ids = jnp.take(ids, order, axis=0)
    ids = jnp.take(ids, (jnp.arange(NX) + x) % NX, axis=1)
    ids = jnp.take(ids, (jnp.arange(2) + core) % 2, axis=2)
    return ids.transpose(3, 2, 1, 0, 4).reshape(CHUNKS, NB * m)


def per_device(
    tokens,
    table,
    gate_weight,
    up_weight,
    down_weight,
    gate_left,
    gate_right,
    up_left,
    up_right,
    down_left,
    down_right,
):
    col = lax.axis_index("col")
    z, y = col // 2, col % 2
    ids = relative_tokens(tokens)

    a, b = gate_left.shape[0], gate_right.shape[1]
    width = gather_small(
        jnp.concatenate([gate_left, up_left, down_right.T], axis=0), "row"
    )
    units = gather_small(
        jnp.concatenate([gate_right.T, up_right.T, down_left], axis=0), "col"
    )
    gate_l, up_l, down_r = (
        width[:, i * a : (i + 1) * a].reshape(-1, width.shape[-1]) for i in range(3)
    )
    gate_r, up_r, down_l = (
        units[:, i * b : (i + 1) * b].reshape(-1, units.shape[-1]) for i in range(3)
    )
    merged_gate = merge_tile(gate_weight, gate_l, gate_r.T)
    merged_up = merge_tile(up_weight, up_l, up_r.T)
    merged_down = merge_tile(down_weight, down_l, down_r.T)
    both = jnp.concatenate([merged_gate, merged_up], axis=1)

    outs = []
    for k in range(CHUNKS):
        embedded = embed(ids[k], table)
        part = jnp.dot(embedded, both, preferred_element_type=F32)
        if k % 2 == 0:
            hidden = swiglu_z_first(part, z, y, 1)
        else:
            hidden = swiglu_y_first(part, z, y, -1)
        outs.append(
            scatter_rows(jnp.dot(hidden, merged_down, preferred_element_type=F32))
        )
    result = jnp.concatenate(outs, axis=0)
    return (result, merged_gate, merged_up, merged_down)


def solution(mesh):
    in_specs = (
        P(),
        P("row", "col"),
        P("col", "row"),
        P("col", "row"),
        P("row", "col"),
        P(("col", "row"), None),
        P(None, ("row", "col")),
        P(("col", "row"), None),
        P(None, ("row", "col")),
        P(("row", "col"), None),
        P(None, ("col", "row")),
    )
    out_specs = (P("row", "col"), P("col", "row"), P("col", "row"), P("row", "col"))
    return jax.shard_map(
        per_device, mesh=mesh, in_specs=in_specs, out_specs=out_specs, check_vma=False
    )
```

time: 572 us -> 203 us (0.35)
  waiting for transfers between devices: 348 us -> 109 us
  blocking collectives: 181 us -> 0 us
  starting transfers between devices: 0.12 us -> 57.5 us
  matrix products: 21.1 us -> 8.36 us
  between operations: 13.8 us -> 1.31 us
  other arithmetic: 3.17 us -> 15.2 us
    psum x2 -> x0, waiting for transfers between devices: 279 us -> none  [the longest x1 270 us: per_device(): gate, up = lax.psum((gate_part, up_part), 'col')]
    all_gather x6 -> x0, blocking collectives: 181 us -> none  [the longest x1 47.1 us: per_device(): lax.all_gather(down_left, 'col', axis=0, tiled=True)]
    ppermute x0 -> x38, waiting for transfers between devices: none -> 109 us  [the longest x16 80.6 us: send_col(): return lax.ppermute(value, 'col', col_perm(**kw))]
    reduce_scatter x1 -> x0, waiting for transfers between devices: 69.1 us -> none  [per_device(): lax.psum_scatter(jnp.dot(hidden, merged_down, preferred_element_type=jnp....]
    ppermute x0 -> x38, starting transfers between devices: none -> 57.5 us  [the longest x16 22.9 us: send_col(): return lax.ppermute(value, 'col', col_perm(**kw))]
    dot_general x6, matrix products: 21.1 us -> 8.36 us  [the longest x1 3.02 us: per_device(): part = jnp.dot(embedded, both, preferred_element_type=F32)]
    convert_element_type x0 -> x5, other arithmetic: none -> 7.01 us  [the longest x3 5.04 us: ring_scatter(): up_next = (block(part, z + d * sign, b) + up).astype(BF16)]
  transfers between devices with their start and end apart: 3 -> 38, of which waited for: 3 -> 24; matrix products, arithmetic and copies ran while one was open for 1% -> 7% of each run, Pallas kernels for 0% -> 0%
where the time goes in v1:
time: 203 us; the launch traced here: 199 us
  waiting for transfers between devices  109 us (54%)
  starting transfers between devices  57.5 us (28%)
  other arithmetic  15.2 us (7%)
  matrix products  8.36 us (4%)
  local copies, waits for them, and re-layouts  7.92 us (4%)
    ppermute x16, waiting for transfers between devices, send_col(): return lax.ppermute(value, 'col', col_perm(**kw))  80.6 us
    ppermute x14, waiting for transfers between devices, send_row(): return lax.ppermute(value, 'row', row_perm(**kw))  23.9 us
    ppermute x16, starting transfers between devices, send_col(): return lax.ppermute(value, 'col', col_perm(**kw))  22.9 us
    ppermute x8, starting transfers between devices, gather_small(): other = lax.ppermute(held, axis, xor_perm(1 << bit))  18.8 us
    ppermute x14, starting transfers between devices, send_row(): return lax.ppermute(value, 'row', row_perm(**kw))  15.9 us
    convert_element_type x3, other arithmetic, ring_scatter(): up_next = (block(part, z + d * sign, b) + up).astype(BF16)  5.04 us
    ppermute x8, waiting for transfers between devices, gather_small(): other = lax.ppermute(held, axis, xor_perm(1 << bit))  4.31 us
  transfers between devices with their start and end apart: 38, of which 24 were waited for; matrix products, arithmetic and copies ran while one was open for 7% of the time, Pallas kernels for 0%

profile of v1, /device:TPU:32, one launch (start us, length us, event | category | flops | bytes accessed | tf_op | source)
XLA Modules:
  0.0 199.1 jit_solution(14596240669687600808)
XLA Ops:
  1.5 3.3 %collective-permute-start.13 = (bf16[1,168,64]{2,1,0:T(8,128)(2,1)S(1)}, bf16[1,168,64]{2,1,0:T(8,128)(2,1)S(1)}, u32[]{:S(2)}, u32[]{:S(2)}) collective-permute-start(bf16[1,168,64]{2,1,0:T(8,128)(2,1)S(1)} %maximum_bitcast_fusion), channel_id=1, source_target_pairs={{0,1},{1,0},{2,3},{3,2},{4,5},{5,4},{6,7},{7,6},{8,9},{9,8},{10,11... | collective-permute-start | bytes 64520 | tf_op jit(solution)/shard_map/ppermute | solution.py:47
  16.6 3.1 %collective-permute-start.11 = (bf16[4,144,64]{2,1,0:T(8,128)(2,1)S(1)}, bf16[4,144,64]{2,1,0:T(8,128)(2,1)S(1)}, u32[]{:S(2)}, u32[]{:S(2)}) collective-permute-start(bf16[4,144,64]{2,1,0:T(8,128)(2,1)S(1)} %pad_maximum_fusion.7), channel_id=1, source_target_pairs={{0,64},{16,80},{32,96},{48,112},{64,0},{80,16},{96,32},{112,48},{1... | collective-permute-start | bytes 221192 | tf_op jit(solution)/shard_map/ppermute | solution.py:47
  19.8 3.4 %collective-permute-start.15 = (bf16[4,168,64]{2,1,0:T(8,128)(2,1)S(1)}, bf16[4,168,64]{2,1,0:T(8,128)(2,1)S(1)}, u32[]{:S(2)}, u32[]{:S(2)}) collective-permute-start(bf16[4,168,64]{2,1,0:T(8,128)(2,1)S(1)} %pad_maximum_fusion.6), channel_id=1, source_target_pairs={{0,4},{1,5},{2,6},{3,7},{4,0},{5,1},{6,2},{7,3},{8,12},{9,13},{10,... | collective-permute-start | bytes 258056 | tf_op jit(solution)/shard_map/ppermute | solution.py:47
  27.1 2.7 %collective-permute-start.2 = (bf16[128,768]{1,0:T(8,128)(2,1)S(1)}, bf16[128,768]{1,0:T(8,128)(2,1)S(1)}, u32[]{:S(2)}, u32[]{:S(2)}) collective-permute-start(bf16[128,768]{1,0:T(8,128)(2,1)S(1)} %get-tuple-element.17), channel_id=1, source_target_pairs={{0,64},{16,80},{32,96},{48,112},{64,0},{80,16},{96,32},{112,48},{1... | collective-permute-start | bytes 589832 | tf_op jit(solution)/shard_map/ppermute | solution.py:36
  31.4 6.4 %collective-permute-start.16 = (bf16[8,168,64]{2,1,0:T(8,128)(2,1)S(1)}, bf16[8,168,64]{2,1,0:T(8,128)(2,1)S(1)}, u32[]{:S(2)}, u32[]{:S(2)}) collective-permute-start(bf16[8,168,64]{2,1,0:T(8,128)(2,1)S(1)} %pad_maximum_fusion.1), channel_id=1, source_target_pairs={{0,8},{1,9},{2,10},{3,11},{4,12},{5,13},{6,14},{7,15},{8,0},{9,1},... | collective-permute-start | bytes 516104 | tf_op jit(solution)/shard_map/ppermute | solution.py:47
  40.2 3.4 %collective-permute-done.4 = bf16[128,768]{1,0:T(8,128)(2,1)S(1)} collective-permute-done((bf16[128,768]{1,0:T(8,128)(2,1)S(1)}, bf16[128,768]{1,0:T(8,128)(2,1)S(1)}, u32[]{:S(2)}, u32[]{:S(2)}) %collective-permute-start.4) | collective-permute-done | bytes 196640 | tf_op jit(solution)/shard_map/ppermute | solution.py:36
  49.4 2.8 %collective-permute-done.6 = bf16[128,768]{1,0:T(8,128)(2,1)S(1)} collective-permute-done((bf16[128,768]{1,0:T(8,128)(2,1)S(1)}, bf16[128,768]{1,0:T(8,128)(2,1)S(1)}, u32[]{:S(2)}, u32[]{:S(2)}) %collective-permute-start.6) | collective-permute-done | bytes 196640 | tf_op jit(solution)/shard_map/ppermute | solution.py:36
  56.7 3.0 %fusion.1 = f32[1024,1792]{1,0:T(8,128)S(1)} fusion(bf16[1024,768]{1,0:T(8,128)(2,1)S(1)} %constant_dynamic-update-slice_fusion, bf16[768,896]{1,0:T(8,128)(2,1)S(1)} %add_convert_fusion.1, bf16[768,896]{1,0:T(8,128)(2,1)S(1)} %add_convert_fusion.2), kind=kOutput, calls=%fused_computation.5 | convolution fusion | flops 2824077312 | bytes 11665408 | tf_op jit(solution)/shard_map/dot_general | solution.py:215
  59.8 2.9 %copy-done.1 = f32[1024,1792]{1,0:T(8,128)} copy-done((f32[1024,1792]{1,0:T(8,128)}, f32[1024,1792]{1,0:T(8,128)S(1)}, u32[]{:S(2)}) %copy-start.1) | copy-done | bytes 7340056
  64.4 11.0 %collective-permute-done.17 = bf16[128,1792]{1,0:T(8,128)(2,1)S(1)} collective-permute-done((bf16[128,1792]{1,0:T(8,128)(2,1)S(1)}, bf16[128,1792]{1,0:T(8,128)(2,1)S(1)}, u32[]{:S(2)}, u32[]{:S(2)}) %collective-permute-start.17) | collective-permute-done | bytes 458784 | tf_op jit(solution)/shard_map/ppermute | solution.py:40
  80.7 10.3 %collective-permute-done.18 = bf16[128,1792]{1,0:T(8,128)(2,1)} collective-permute-done((bf16[128,1792]{1,0:T(8,128)(2,1)S(1)}, bf16[128,1792]{1,0:T(8,128)(2,1)}, u32[]{:S(2)}, u32[]{:S(2)}) %collective-permute-start.18) | collective-permute-done | bytes 458784 | tf_op jit(solution)/shard_map/ppermute | solution.py:40
  92.5 12.3 %collective-permute-done.19 = bf16[128,1792]{1,0:T(8,128)(2,1)S(1)} collective-permute-done((bf16[128,1792]{1,0:T(8,128)(2,1)S(1)}, bf16[128,1792]{1,0:T(8,128)(2,1)S(1)}, u32[]{:S(2)}, u32[]{:S(2)}) %collective-permute-start.19) | collective-permute-done | bytes 458784 | tf_op jit(solution)/shard_map/ppermute | solution.py:40
  107.2 3.0 %collective-permute-start.22 = (bf16[128,1792]{1,0:T(8,128)(2,1)}, bf16[128,1792]{1,0:T(8,128)(2,1)S(1)}, u32[]{:S(2)}, u32[]{:S(2)}) collective-permute-start(bf16[128,1792]{1,0:T(8,128)(2,1)} %get-tuple-element.9), channel_id=1, source_target_pairs={{0,14},{1,15},{2,0},{3,1},{4,2},{5,3},{6,4},{7,5},{8,6},{9,7},{10,... | collective-permute-start | bytes 1376264 | tf_op jit(solution)/shard_map/ppermute | solution.py:40
  110.1 8.1 %collective-permute-done.22 = bf16[128,1792]{1,0:T(8,128)(2,1)S(1)} collective-permute-done((bf16[128,1792]{1,0:T(8,128)(2,1)}, bf16[128,1792]{1,0:T(8,128)(2,1)S(1)}, u32[]{:S(2)}, u32[]{:S(2)}) %collective-permute-start.22) | collective-permute-done | bytes 458784 | tf_op jit(solution)/shard_map/ppermute | solution.py:40
  121.9 7.0 %collective-permute-done.23 = bf16[128,1792]{1,0:T(8,128)(2,1)} collective-permute-done((bf16[128,1792]{1,0:T(8,128)(2,1)S(1)}, bf16[128,1792]{1,0:T(8,128)(2,1)}, u32[]{:S(2)}, u32[]{:S(2)}) %collective-permute-start.23) | collective-permute-done | bytes 458784 | tf_op jit(solution)/shard_map/ppermute | solution.py:40
  132.4 5.7 %collective-permute-done.24 = bf16[64,1792]{1,0:T(8,128)(2,1)S(1)} collective-permute-done((bf16[64,1792]{1,0:T(8,128)(2,1)S(1)}, bf16[64,1792]{1,0:T(8,128)(2,1)S(1)}, u32[]{:S(2)}, u32[]{:S(2)}) %collective-permute-start.24) | collective-permute-done | bytes 229408 | tf_op jit(solution)/shard_map/ppermute | solution.py:40
  140.7 4.6 %collective-permute-done.25 = bf16[64,896]{1,0:T(8,128)(2,1)S(1)} collective-permute-done((bf16[64,896]{1,0:T(8,128)(2,1)}, bf16[64,896]{1,0:T(8,128)(2,1)S(1)}, u32[]{:S(2)}, u32[]{:S(2)}) %collective-permute-start.25) | collective-permute-done | bytes 114720 | tf_op jit(solution)/shard_map/ppermute | solution.py:40
  148.8 5.1 %collective-permute-done.26 = bf16[128,896]{1,0:T(8,128)(2,1)S(1)} collective-permute-done((bf16[128,896]{1,0:T(8,128)(2,1)S(1)}, bf16[128,896]{1,0:T(8,128)(2,1)S(1)}, u32[]{:S(2)}, u32[]{:S(2)}) %collective-permute-start.26) | collective-permute-done | bytes 229408 | tf_op jit(solution)/shard_map/ppermute | solution.py:40
  156.9 4.9 %collective-permute-done.28 = bf16[128,896]{1,0:T(8,128)(2,1)S(1)} collective-permute-done((bf16[128,896]{1,0:T(8,128)(2,1)S(1)}, bf16[128,896]{1,0:T(8,128)(2,1)S(1)}, u32[]{:S(2)}, u32[]{:S(2)}) %collective-permute-start.28) | collective-permute-done | bytes 229408 | tf_op jit(solution)/shard_map/ppermute | solution.py:40
  161.8 3.0 %collective-permute-start.31 = (bf16[128,896]{1,0:T(8,128)(2,1)S(1)}, bf16[128,896]{1,0:T(8,128)(2,1)S(1)}, u32[]{:S(2)}, u32[]{:S(2)}) collective-permute-start(bf16[128,896]{1,0:T(8,128)(2,1)S(1)} %collective-permute-done.29), channel_id=1, source_target_pairs={{0,14},{1,15},{2,0},{3,1},{4,2},{5,3},{6,4},{7,5},{8,6},{9,7},{10,... | collective-permute-start | bytes 688136 | tf_op jit(solution)/shard_map/ppermute | solution.py:40
  164.8 3.9 %collective-permute-done.30 = bf16[128,896]{1,0:T(8,128)(2,1)S(1)} collective-permute-done((bf16[128,896]{1,0:T(8,128)(2,1)S(1)}, bf16[128,896]{1,0:T(8,128)(2,1)S(1)}, u32[]{:S(2)}, u32[]{:S(2)}) %collective-permute-start.30) | collective-permute-done | bytes 229408 | tf_op jit(solution)/shard_map/ppermute | solution.py:40
  168.8 7.1 %collective-permute-done.32 = bf16[128,896]{1,0:T(8,128)(2,1)S(1)} collective-permute-done((bf16[128,896]{1,0:T(8,128)(2,1)S(1)}, bf16[128,896]{1,0:T(8,128)(2,1)S(1)}, u32[]{:S(2)}, u32[]{:S(2)}) %collective-permute-start.32) | collective-permute-done | bytes 229408 | tf_op jit(solution)/shard_map/ppermute | solution.py:40
  184.3 8.6 %collective-permute-done.34 = bf16[128,768]{1,0:T(8,128)(2,1)S(1)} collective-permute-done((bf16[128,768]{1,0:T(8,128)(2,1)S(1)}, bf16[128,768]{1,0:T(8,128)(2,1)S(1)}, u32[]{:S(2)}, u32[]{:S(2)}) %collective-permute-start.34) | collective-permute-done | bytes 196640 | tf_op jit(solution)/shard_map/ppermute | solution.py:36
  195.2 3.2 %collective-permute-done.37 = bf16[64,768]{1,0:T(8,128)(2,1)S(1)} collective-permute-done((bf16[64,768]{1,0:T(8,128)(2,1)S(1)}, bf16[64,768]{1,0:T(8,128)(2,1)S(1)}, u32[]{:S(2)}, u32[]{:S(2)}) %collective-permute-start.37) | collective-permute-done | bytes 98336 | tf_op jit(solution)/shard_map/ppermute | solution.py:36
  (162 shorter events, 68.9 us)
Async XLA Ops:
  1.5 12.2 %collective-permute-start.13 = (bf16[1,168,64]{2,1,0:T(8,128)(2,1)S(1)}, bf16[1,168,64]{2,1,0:T(8,128)(2,1)S(1)}, u32[]{:S(2)}, u32[]{:S(2)}) collective-permute-start(bf16[1,168,64]{2,1,0:T(8,128)(2,1)S(1)} %maximum_bitcast_fusion), channel_id=1, source_target_pairs={{0,1},{1,0},{2,3},{3,2},{4,5},{5,4},{6,7},{7,6},{8,9},{9,8},{10,11... | collective-permute-start | bytes 64520 | tf_op jit(solution)/shard_map/ppermute | solution.py:47
  11.6 12.7 %collective-permute-start = (bf16[512,768]{1,0:T(8,128)(2,1)}, bf16[512,768]{1,0:T(8,128)(2,1)}, u32[]{:S(2)}, u32[]{:S(2)}) collective-permute-start(bf16[512,768]{1,0:T(8,128)(2,1)} %slice.108), channel_id=1, source_target_pairs={{0,16},{16,0},{32,48},{48,32},{64,80},{80,64},{96,112},{112,96},{1... | collective-permute-start | bytes 2359304 | tf_op jit(solution)/shard_map/ppermute | solution.py:36
  19.8 11.4 %collective-permute-start.15 = (bf16[4,168,64]{2,1,0:T(8,128)(2,1)S(1)}, bf16[4,168,64]{2,1,0:T(8,128)(2,1)S(1)}, u32[]{:S(2)}, u32[]{:S(2)}) collective-permute-start(bf16[4,168,64]{2,1,0:T(8,128)(2,1)S(1)} %pad_maximum_fusion.6), channel_id=1, source_target_pairs={{0,4},{1,5},{2,6},{3,7},{4,0},{5,1},{6,2},{7,3},{8,12},{9,13},{10,... | collective-permute-start | bytes 258056 | tf_op jit(solution)/shard_map/ppermute | solution.py:47
  23.5 15.8 %collective-permute-start.12 = (bf16[8,144,64]{2,1,0:T(8,128)(2,1)S(1)}, bf16[8,144,64]{2,1,0:T(8,128)(2,1)S(1)}, u32[]{:S(2)}, u32[]{:S(2)}) collective-permute-start(bf16[8,144,64]{2,1,0:T(8,128)(2,1)S(1)} %pad_maximum_fusion.2), channel_id=1, source_target_pairs={{0,128},{16,144},{32,160},{48,176},{64,192},{80,208},{96,224},{112... | collective-permute-start | bytes 442376 | tf_op jit(solution)/shard_map/ppermute | solution.py:47
  25.5 12.3 %collective-permute-start.1 = (bf16[128,768]{1,0:T(8,128)(2,1)S(1)}, bf16[128,768]{1,0:T(8,128)(2,1)S(1)}, u32[]{:S(2)}, u32[]{:S(2)}) collective-permute-start(bf16[128,768]{1,0:T(8,128)(2,1)S(1)} %get-tuple-element.15), channel_id=1, source_target_pairs={{0,32},{16,48},{32,64},{48,80},{64,96},{80,112},{96,0},{112,16},{1... | collective-permute-start | bytes 589832 | tf_op jit(solution)/shard_map/ppermute | solution.py:36
  27.1 10.7 %collective-permute-start.2 = (bf16[128,768]{1,0:T(8,128)(2,1)S(1)}, bf16[128,768]{1,0:T(8,128)(2,1)S(1)}, u32[]{:S(2)}, u32[]{:S(2)}) collective-permute-start(bf16[128,768]{1,0:T(8,128)(2,1)S(1)} %get-tuple-element.17), channel_id=1, source_target_pairs={{0,64},{16,80},{32,96},{48,112},{64,0},{80,16},{96,32},{112,48},{1... | collective-permute-start | bytes 589832 | tf_op jit(solution)/shard_map/ppermute | solution.py:36
  29.8 8.0 %collective-permute-start.3 = (bf16[128,768]{1,0:T(8,128)(2,1)S(1)}, bf16[128,768]{1,0:T(8,128)(2,1)S(1)}, u32[]{:S(2)}, u32[]{:S(2)}) collective-permute-start(bf16[128,768]{1,0:T(8,128)(2,1)S(1)} %get-tuple-element.16), channel_id=1, source_target_pairs={{0,96},{16,112},{32,0},{48,16},{64,32},{80,48},{96,64},{112,80},{1... | collective-permute-start | bytes 589832 | tf_op jit(solution)/shard_map/ppermute | solution.py:36
  31.4 16.6 %collective-permute-start.16 = (bf16[8,168,64]{2,1,0:T(8,128)(2,1)S(1)}, bf16[8,168,64]{2,1,0:T(8,128)(2,1)S(1)}, u32[]{:S(2)}, u32[]{:S(2)}) collective-permute-start(bf16[8,168,64]{2,1,0:T(8,128)(2,1)S(1)} %pad_maximum_fusion.1), channel_id=1, source_target_pairs={{0,8},{1,9},{2,10},{3,11},{4,12},{5,13},{6,14},{7,15},{8,0},{9,1},... | collective-permute-start | bytes 516104 | tf_op jit(solution)/shard_map/ppermute | solution.py:47
  44.9 7.3 %collective-permute-start.6 = (bf16[128,768]{1,0:T(8,128)(2,1)S(1)}, bf16[128,768]{1,0:T(8,128)(2,1)S(1)}, u32[]{:S(2)}, u32[]{:S(2)}) collective-permute-start(bf16[128,768]{1,0:T(8,128)(2,1)S(1)} %get-tuple-element.7), channel_id=1, source_target_pairs={{0,64},{16,80},{32,96},{48,112},{64,0},{80,16},{96,32},{112,48},{1... | collective-permute-start | bytes 589832 | tf_op jit(solution)/shard_map/ppermute | solution.py:36
  46.4 7.8 %collective-permute-start.7 = (bf16[128,768]{1,0:T(8,128)(2,1)S(1)}, bf16[128,768]{1,0:T(8,128)(2,1)S(1)}, u32[]{:S(2)}, u32[]{:S(2)}) collective-permute-start(bf16[128,768]{1,0:T(8,128)(2,1)S(1)} %get-tuple-element.7), channel_id=1, source_target_pairs={{0,32},{16,48},{32,64},{48,80},{64,96},{80,112},{96,0},{112,16},{1... | collective-permute-start | bytes 589832 | tf_op jit(solution)/shard_map/ppermute | solution.py:36
  62.8 12.6 %collective-permute-start.17 = (bf16[128,1792]{1,0:T(8,128)(2,1)S(1)}, bf16[128,1792]{1,0:T(8,128)(2,1)S(1)}, u32[]{:S(2)}, u32[]{:S(2)}) collective-permute-start(bf16[128,1792]{1,0:T(8,128)(2,1)S(1)} %get-tuple-element.10), channel_id=1, source_target_pairs={{0,2},{1,3},{2,4},{3,5},{4,6},{5,7},{6,8},{7,9},{8,10},{9,11},{10,... | collective-permute-start | bytes 1376264 | tf_op jit(solution)/shard_map/ppermute | solution.py:40
  76.7 14.3 %collective-permute-start.18 = (bf16[128,1792]{1,0:T(8,128)(2,1)S(1)}, bf16[128,1792]{1,0:T(8,128)(2,1)}, u32[]{:S(2)}, u32[]{:S(2)}) collective-permute-start(bf16[128,1792]{1,0:T(8,128)(2,1)S(1)} %add_convert_fusion.7), channel_id=1, source_target_pairs={{0,2},{1,3},{2,4},{3,5},{4,6},{5,7},{6,8},{7,9},{8,10},{9,11},{10,... | collective-permute-start | bytes 1376264 | tf_op jit(solution)/shard_map/ppermute | solution.py:40
  78.3 14.3 %collective-permute-start.21 = (bf16[128,1792]{1,0:T(8,128)(2,1)S(1)}, bf16[128,1792]{1,0:T(8,128)(2,1)S(1)}, u32[]{:S(2)}, u32[]{:S(2)}) collective-permute-start(bf16[128,1792]{1,0:T(8,128)(2,1)S(1)} %get-tuple-element.11), channel_id=1, source_target_pairs={{0,14},{1,15},{2,0},{3,1},{4,2},{5,3},{6,4},{7,5},{8,6},{9,7},{10,... | collective-permute-start | bytes 1376264 | tf_op jit(solution)/shard_map/ppermute | solution.py:40
  92.4 12.4 %collective-permute-start.19 = (bf16[128,1792]{1,0:T(8,128)(2,1)S(1)}, bf16[128,1792]{1,0:T(8,128)(2,1)S(1)}, u32[]{:S(2)}, u32[]{:S(2)}) collective-permute-start(bf16[128,1792]{1,0:T(8,128)(2,1)S(1)} %add_convert_fusion.6), channel_id=1, source_target_pairs={{0,2},{1,3},{2,4},{3,5},{4,6},{5,7},{6,8},{7,9},{8,10},{9,11},{10,... | collective-permute-start | bytes 1376264 | tf_op jit(solution)/shard_map/ppermute | solution.py:40
  107.2 11.0 %collective-permute-start.22 = (bf16[128,1792]{1,0:T(8,128)(2,1)}, bf16[128,1792]{1,0:T(8,128)(2,1)S(1)}, u32[]{:S(2)}, u32[]{:S(2)}) collective-permute-start(bf16[128,1792]{1,0:T(8,128)(2,1)} %get-tuple-element.9), channel_id=1, source_target_pairs={{0,14},{1,15},{2,0},{3,1},{4,2},{5,3},{6,4},{7,5},{8,6},{9,7},{10,... | collective-permute-start | bytes 1376264 | tf_op jit(solution)/shard_map/ppermute | solution.py:40
  110.1 11.8 %collective-permute-start.20 = (bf16[128,1792]{1,0:T(8,128)(2,1)S(1)}, bf16[128,1792]{1,0:T(8,128)(2,1)S(1)}, u32[]{:S(2)}, u32[]{:S(2)}) collective-permute-start(bf16[128,1792]{1,0:T(8,128)(2,1)S(1)} %get-tuple-element.8), channel_id=1, source_target_pairs={{0,2},{1,3},{2,4},{3,5},{4,6},{5,7},{6,8},{7,9},{8,10},{9,11},{10,... | collective-permute-start | bytes 1376264 | tf_op jit(solution)/shard_map/ppermute | solution.py:40
  119.5 9.5 %collective-permute-start.23 = (bf16[128,1792]{1,0:T(8,128)(2,1)S(1)}, bf16[128,1792]{1,0:T(8,128)(2,1)}, u32[]{:S(2)}, u32[]{:S(2)}) collective-permute-start(bf16[128,1792]{1,0:T(8,128)(2,1)S(1)} %add_convert_fusion.3), channel_id=1, source_target_pairs={{0,14},{1,15},{2,0},{3,1},{4,2},{5,3},{6,4},{7,5},{8,6},{9,7},{10,... | collective-permute-start | bytes 1376264 | tf_op jit(solution)/shard_map/ppermute | solution.py:40
  130.4 7.7 %collective-permute-start.24 = (bf16[64,1792]{1,0:T(8,128)(2,1)S(1)}, bf16[64,1792]{1,0:T(8,128)(2,1)S(1)}, u32[]{:S(2)}, u32[]{:S(2)}) collective-permute-start(bf16[64,1792]{1,0:T(8,128)(2,1)S(1)} %dynamic-slice_convert_fusion.2), channel_id=1, source_target_pairs={{0,1},{1,0},{2,3},{3,2},{4,5},{5,4},{6,7},{7,6},{8,9},{9,8},{10,11... | collective-permute-start | bytes 688136 | tf_op jit(solution)/shard_map/ppermute | solution.py:40
  145.7 8.2 %collective-permute-start.26 = (bf16[128,896]{1,0:T(8,128)(2,1)S(1)}, bf16[128,896]{1,0:T(8,128)(2,1)S(1)}, u32[]{:S(2)}, u32[]{:S(2)}) collective-permute-start(bf16[128,896]{1,0:T(8,128)(2,1)S(1)} %get-tuple-element.32), channel_id=1, source_target_pairs={{0,2},{1,3},{2,4},{3,5},{4,6},{5,7},{6,8},{7,9},{8,10},{9,11},{10,... | collective-permute-start | bytes 688136 | tf_op jit(solution)/shard_map/ppermute | solution.py:40
  147.5 7.4 %collective-permute-start.27 = (bf16[128,896]{1,0:T(8,128)(2,1)S(1)}, bf16[128,896]{1,0:T(8,128)(2,1)S(1)}, u32[]{:S(2)}, u32[]{:S(2)}) collective-permute-start(bf16[128,896]{1,0:T(8,128)(2,1)S(1)} %get-tuple-element.32), channel_id=1, source_target_pairs={{0,14},{1,15},{2,0},{3,1},{4,2},{5,3},{6,4},{7,5},{8,6},{9,7},{10,... | collective-permute-start | bytes 688136 | tf_op jit(solution)/shard_map/ppermute | solution.py:40
  153.9 7.9 %collective-permute-start.28 = (bf16[128,896]{1,0:T(8,128)(2,1)S(1)}, bf16[128,896]{1,0:T(8,128)(2,1)S(1)}, u32[]{:S(2)}, u32[]{:S(2)}) collective-permute-start(bf16[128,896]{1,0:T(8,128)(2,1)S(1)} %collective-permute-done.26), channel_id=1, source_target_pairs={{0,2},{1,3},{2,4},{3,5},{4,6},{5,7},{6,8},{7,9},{8,10},{9,11},{10,... | collective-permute-start | bytes 688136 | tf_op jit(solution)/shard_map/ppermute | solution.py:40
  180.5 12.4 %collective-permute-start.34 = (bf16[128,768]{1,0:T(8,128)(2,1)S(1)}, bf16[128,768]{1,0:T(8,128)(2,1)S(1)}, u32[]{:S(2)}, u32[]{:S(2)}) collective-permute-start(bf16[128,768]{1,0:T(8,128)(2,1)S(1)} %get-tuple-element.12), channel_id=1, source_target_pairs={{0,32},{16,48},{32,64},{48,80},{64,96},{80,112},{96,0},{112,16},{1... | collective-permute-start | bytes 589832 | tf_op jit(solution)/shard_map/ppermute | solution.py:36
  180.6 12.4 %collective-permute-start.35 = (bf16[128,768]{1,0:T(8,128)(2,1)S(1)}, bf16[128,768]{1,0:T(8,128)(2,1)S(1)}, u32[]{:S(2)}, u32[]{:S(2)}) collective-permute-start(bf16[128,768]{1,0:T(8,128)(2,1)S(1)} %get-tuple-element.14), channel_id=1, source_target_pairs={{0,64},{16,80},{32,96},{48,112},{64,0},{80,16},{96,32},{112,48},{1... | collective-permute-start | bytes 589832 | tf_op jit(solution)/shard_map/ppermute | solution.py:36
  182.6 11.0 %collective-permute-start.36 = (bf16[128,768]{1,0:T(8,128)(2,1)S(1)}, bf16[128,768]{1,0:T(8,128)(2,1)S(1)}, u32[]{:S(2)}, u32[]{:S(2)}) collective-permute-start(bf16[128,768]{1,0:T(8,128)(2,1)S(1)} %get-tuple-element.13), channel_id=1, source_target_pairs={{0,96},{16,112},{32,0},{48,16},{64,32},{80,48},{96,64},{112,80},{1... | collective-permute-start | bytes 589832 | tf_op jit(solution)/shard_map/ppermute | solution.py:36
  (30 other events, 181.1 us)
